TPU v7x, 32 devices: a whole 2x2x4 slice. The times are simulated.
32 devices in a mesh: grp: 2 (over x), row: 16 (over z, y, core).
Axes of the slice: x: 2, y: 2, z: 4, core: 2. Of those that a mesh axis runs over, the one named last changes fastest.
Arguments:
- amplitudes: bfloat16 [12288, 6144], P(('grp', 'row')), parts along dimension 0, may hold values from -6 to 6
- integrals: bfloat16 [12288, 6144], P(('grp', 'row')), parts along dimension 0, may hold values from -0.078125 to 0.078125
- occupied_energy: float32 [96], replicated, may hold values from 0.3 to 3
- virtual_energy: float32 [8, 64], replicated, may hold values from 0.05 to 4
- pair_irrep: int32 [192], P('grp'), parts along dimension 0, may hold values from 0 to 7
Outputs:
- increment: bfloat16 [12288, 6144], P(('grp', 'row')), parts along dimension 0
There are 2 independent parts, one for each index of `grp`. A program takes and returns all parts, laid end to end along the dimension named above; an argument that names none is the same for every part. Nothing has to cross between parts.
All inputs are finite; a program needn't handle non-finite values.
Results may differ from a plain program's by a relative error of at most 0.001.
Values may be sent and summed in bfloat16 or wider, within the bound.
A program may use at most 192 MiB of HBM per device.

v0:
```python
import jax
import jax.numpy as jnp
from jax import lax
from jax.sharding import PartitionSpec as P


def pair_energies(occupied_energy, virtual_energy, pair_irrep):
    labels = jnp.arange(virtual_energy.shape[0])
    onehot = (pair_irrep[:, None] == labels[None, :]).astype(jnp.float32)
    virtual = jnp.sum(onehot[:, :, None] * virtual_energy[None, :, :], axis=1)
    return (virtual + occupied_energy[:, None]).reshape(-1)


def shards(amplitudes, integrals, occupied_energy, virtual_energy, pair_irrep):
    devices = lax.axis_size("row")
    position = lax.axis_index("row")
    levels = devices.bit_length() - 1
    layer_bits = 0
    panel_bits = (levels - layer_bits) // 2
    block_bits = levels - layer_bits - panel_bits
    panel_count = 1 << panel_bits
    block_count = 1 << block_bits
    layer_count = 1 << layer_bits
    local_rows = amplitudes.shape[0]
    columns = amplitudes.shape[1]
    panel_rows = local_rows // panel_count
    layer_rows = local_rows // layer_count
    block_cols = columns // block_count
    own_panel = position % panel_count
    own_block = position // panel_count % block_count
    reshaped = amplitudes.reshape(panel_count, panel_rows, devices, layer_count, layer_rows)
    reshaped = jnp.transpose(reshaped, (3, 0, 1, 2, 4))
    outgoing = jnp.broadcast_to(
        reshaped[:, None], (layer_count, block_count, panel_count, panel_rows, devices, layer_rows)
    )
    outgoing = outgoing.reshape(devices, panel_rows, devices * layer_rows)
    row_panel = lax.all_to_all(outgoing, "row", split_axis=0, concat_axis=0, tiled=True)
    row_panel = row_panel.reshape(devices * panel_rows, devices * layer_rows)
    tile_blocks = integrals.reshape(layer_count, layer_rows, block_count, block_cols)
    tile_blocks = jnp.transpose(tile_blocks, (0, 2, 1, 3))
    tile_out = jnp.broadcast_to(
        tile_blocks[:, :, None], (layer_count, block_count, panel_count, layer_rows, block_cols)
    )
    tile_out = tile_out.reshape(devices, layer_rows, block_cols)
    integral_slab = lax.all_to_all(tile_out, "row", split_axis=0, concat_axis=0, tiled=True)
    integral_slab = integral_slab.reshape(devices * layer_rows, block_cols)
    partial_value = jnp.dot(row_panel, integral_slab, preferred_element_type=jnp.float32)
    pair_energy = pair_energies(occupied_energy, virtual_energy, pair_irrep)
    current = partial_value.reshape(devices, panel_rows, block_cols)
    row_energy = lax.dynamic_slice_in_dim(
        pair_energy.reshape(devices, panel_count, panel_rows), own_panel, 1, 1
    )
    row_energy = row_energy.reshape(devices, panel_rows, 1)
    col_energy = lax.dynamic_slice_in_dim(pair_energy, own_block * block_cols, block_cols)
    finished = (current / (row_energy + col_energy[None, None, :])).astype(jnp.bfloat16)
    arrived = lax.all_to_all(finished, "row", split_axis=0, concat_axis=0, tiled=True)
    arranged = arrived.reshape(block_count, panel_count, panel_rows, block_cols)
    arranged = jnp.transpose(arranged, (1, 2, 0, 3))
    return arranged.reshape(local_rows, columns)


def solution(mesh):
    in_specs = (P(("grp", "row"), None), P(("grp", "row"), None), P(), P(), P("grp"))
    out_specs = P(("grp", "row"), None)
    return jax.shard_map(shards, mesh=mesh, in_specs=in_specs, out_specs=out_specs, check_vma=False)
```

profile of v0, /device:TPU:0, one launch (start us, length us, event | category | flops | bytes accessed | tf_op | source)
XLA Modules:
  0.0 1025.5 jit_solution(2003462270804955537)
XLA Ops:
  0.0 3.5 copy.14
  3.5 7.1 broadcast_in_dim.26
  10.6 27.0 %broadcast_in_dim.27 = bf16[16,96,6144]{2,1,0:T(8,128)(2,1)} reshape(bf16[4,4,96,16,384]{4,3,2,1,0:T(8,128)(2,1)} %broadcast_in_dim.26) | data formatting | bytes 37748736 | tf_op jit(solution)/shard_map/broadcast_in_dim | solution.py:33
  37.5 7.4 all-to-all-start
  45.0 8.2 reshape.60
  53.2 5.4 copy.10
  58.6 319.7 %all-to-all-done = bf16[16,96,6144]{2,1,0:T(8,128)(2,1)} async-done(((bf16[16,96,6144]{2,1,0:T(8,128)(2,1)}), bf16[16,96,6144]{2,1,0:T(8,128)(2,1)}, u32[]{:S(2)}, u32[]{:S(2)}) %all-to-all-start) | async-done | bytes 18874400 | tf_op jit(solution)/shard_map/all_to_all | solution.py:37
  378.3 8.3 broadcast_in_dim.29
  386.6 0.0 copy-start.2
  386.6 0.0 copy-start
  386.6 78.8 %all-to-all-start.1 = ((bf16[16,384,1536]{2,1,0:T(8,128)(2,1)}), bf16[16,384,1536]{2,1,0:T(8,128)(2,1)}, u32[]{:S(2)}, u32[]{:S(2)}) async-start(bf16[16,384,1536]{2,1,0:T(8,128)(2,1)} %bitcast.21), calls=%async_computation.1 | async-start | bytes 37748736 | tf_op jit(solution)/shard_map/all_to_all | solution.py:45
  465.4 0.0 copy-done.2
  465.4 0.0 copy-done
  465.4 0.1 multiply_reduce_fusion
  465.6 0.0 copy-done.1
  465.6 0.1 copy.11
  465.7 0.1 add.52
  465.8 0.1 add.47
  465.9 0.1 dynamic_slice.7
  466.0 332.7 %all-to-all-done.1 = bf16[16,384,1536]{2,1,0:T(8,128)(2,1)} async-done(((bf16[16,384,1536]{2,1,0:T(8,128)(2,1)}), bf16[16,384,1536]{2,1,0:T(8,128)(2,1)}, u32[]{:S(2)}, u32[]{:S(2)}) %all-to-all-start.1) | async-done | bytes 18874400 | tf_op jit(solution)/shard_map/all_to_all | solution.py:45
  798.7 37.8 %divide_convert_fusion = bf16[16,96,1536]{2,1,0:T(8,128)(2,1)S(1)} fusion(bf16[16,96,6144]{2,1,0:T(8,128)(2,1)} %all-to-all-done, bf16[6144,1536,1]{1,0,2:T(8,128)(2,1)} %bitcast.4, f32[1536]{0:T(1024)S(1)} %dynamic_slice.7, f32[16,96]{1,0:T(8,128)S(1)} %bitcast.27), kind=kOutput, calls=%fused_computation | convolution fusion | flops 28998107136 | bytes 42479616 | tf_op jit(solution)/shard_map/dot_general | solution.py:47
  836.5 181.9 %all_to_all.15 = bf16[16,96,1536]{2,1,0:T(8,128)(2,1)S(1)} all-to-all(bf16[16,96,1536]{2,1,0:T(8,128)(2,1)S(1)} %divide_convert_fusion), channel_id=1, replica_groups=mesh['grp'=2,'row'=16] {'row'}, dimensions={0} | all-to-all | bytes 9437184 | tf_op jit(solution)/shard_map/all_to_all | solution.py:56
  1018.4 3.6 copy.13
  1022.0 3.5 copy.15
  (4 shorter events, 0.0 us)
Async XLA Ops:
  37.5 340.7 %all-to-all-start = ((bf16[16,96,6144]{2,1,0:T(8,128)(2,1)}), bf16[16,96,6144]{2,1,0:T(8,128)(2,1)}, u32[]{:S(2)}, u32[]{:S(2)}) async-start(bf16[16,96,6144]{2,1,0:T(8,128)(2,1)} %broadcast_in_dim.27), calls=%async_computation | async-start | bytes 37748736 | tf_op jit(solution)/shard_map/all_to_all | solution.py:37
  386.6 78.9 %copy-start.2 = (s32[96]{0:T(128)S(1)}, s32[96]{0:T(128)}, u32[]{:S(2)}) copy-start(s32[96]{0:T(128)} %param.9) | copy-start | bytes 1156
  386.6 78.9 %copy-start = (f32[8,64]{1,0:T(8,128)S(1)}, f32[8,64]{1,0:T(8,128)}, u32[]{:S(2)}) copy-start(f32[8,64]{1,0:T(8,128)} %param.8) | copy-start | bytes 6148
  386.6 79.0 %copy-start.1 = (f32[96]{0:T(128)S(1)}, f32[96]{0:T(128)}, u32[]{:S(2)}) copy-start(f32[96]{0:T(128)} %param.7) | copy-start | bytes 1156
  386.6 412.1 %all-to-all-start.1 = ((bf16[16,384,1536]{2,1,0:T(8,128)(2,1)}), bf16[16,384,1536]{2,1,0:T(8,128)(2,1)}, u32[]{:S(2)}, u32[]{:S(2)}) async-start(bf16[16,384,1536]{2,1,0:T(8,128)(2,1)} %bitcast.21), calls=%async_computation.1 | async-start | bytes 37748736 | tf_op jit(solution)/shard_map/all_to_all | solution.py:45
where the time goes:
time: 1030 us
  waiting for transfers between devices  652 us (63%)
  blocking collectives  182 us (18%)
  starting transfers between devices  86.2 us (8%)
  local copies, waits for them, and re-layouts  66.9 us (6%)
  matrix products  37.8 us (4%)
    all_to_all x1, waiting for transfers between devices, shards(): lax.all_to_all(tile_out, 'row', split_axis=0, concat_axis=0, tiled=True)  333 us
    all_to_all x1, waiting for transfers between devices, shards(): lax.all_to_all(outgoing, 'row', split_axis=0, concat_axis=0, tiled=True)  320 us
    all_to_all x1, blocking collectives, shards(): lax.all_to_all(finished, 'row', split_axis=0, concat_axis=0, tiled=True)  182 us
    all_to_all x1, starting transfers between devices, shards(): lax.all_to_all(tile_out, 'row', split_axis=0, concat_axis=0, tiled=True)  78.8 us
    dot_general x1, matrix products, shards(): jnp.dot(row_panel, integral_slab, preferred_element_type=jnp.float32)  37.8 us
    broadcast_in_dim x2, local copies, waits for them, and re-layouts, shards(): jnp.broadcast_to(reshaped[:, None], (layer_count, block_count, panel_coun...  34.1 us
  transfers between devices with their start and end apart: 2, of which 2 were waited for; matrix products, arithmetic and copies ran while one was open for 1% of the time, Pallas kernels for 0%

commit v1 on v0

v1 whole, which is shorter than its diff:
```python
import functools
import jax
import jax.numpy as jnp
from jax import lax
from jax.experimental import pallas as pl
from jax.experimental.pallas import tpu as pltpu
from jax.sharding import PartitionSpec as P

QUAD = 4
MESH = pl.DeviceIdType.MESH


def pair_energies(occupied_energy, virtual_energy, pair_irrep):
    labels = jnp.arange(virtual_energy.shape[0])
    onehot = (pair_irrep[:, None] == labels[None, :]).astype(jnp.float32)
    virtual = jnp.sum(onehot[:, :, None] * virtual_energy[None, :, :], axis=1)
    return (virtual + occupied_energy[:, None]).reshape(-1)


def kernel(layers, chunks, a_ref, b_ref, row_ref, col_ref, out_ref, a_all, b_all, c_all,
           local_sem, bq_send, bq_recv, a_send, a_recv, z_send, z_recv, c_send, c_recv, c_local):
    rows = a_ref.shape[0]
    width = b_all.shape[2]
    quarter = chunks * width
    layer_rows = QUAD * rows
    me = lax.axis_index("row")
    layer, spot = me // QUAD, me % QUAD
    half, core = spot // 2, spot % 2
    spots = ((half * 2) + (1 - core), (1 - half) * 2 + core, (1 - half) * 2 + (1 - core))
    peers = [layer * QUAD + s for s in spots]
    first = layer * QUAD
    has_below, has_above = layer > 0, layer < layers - 1

    def local_a():
        return pltpu.make_async_copy(a_ref, a_all.at[spot], local_sem.at[0])

    def cols(owner, c):
        return pl.ds(pl.multiple_of(owner * quarter + c * width, width), width)

    def local_b(c):
        return pltpu.make_async_copy(
            b_ref.at[:, cols(spot, c)], b_all.at[c, pl.ds(me * rows, rows), :], local_sem.at[1 + c])

    def quad_b(c, p):
        return pltpu.make_async_remote_copy(
            src_ref=b_ref.at[:, cols(spots[p], c)], dst_ref=b_all.at[c, pl.ds(me * rows, rows), :],
            send_sem=bq_send.at[c, p], recv_sem=bq_recv.at[c, p],
            device_id={"row": peers[p]}, device_id_type=MESH)

    def quad_a(p):
        if p == 2:
            return pltpu.make_async_remote_copy(
                src_ref=a_all.at[spots[1]], dst_ref=a_all.at[spots[1]],
                send_sem=a_send.at[p], recv_sem=a_recv.at[p],
                device_id={"row": peers[0]}, device_id_type=MESH)
        return pltpu.make_async_remote_copy(
            src_ref=a_ref, dst_ref=a_all.at[spot],
            send_sem=a_send.at[p], recv_sem=a_recv.at[p],
            device_id={"row": peers[p]}, device_id_type=MESH)

    def along(c, owner, up):
        block = b_all.at[c, pl.ds(owner * layer_rows, layer_rows), :]
        return pltpu.make_async_remote_copy(
            src_ref=block, dst_ref=block,
            send_sem=z_send.at[up, c, owner], recv_sem=z_recv.at[c, owner],
            device_id={"row": me + QUAD if up else me - QUAD}, device_id_type=MESH)

    def result(c, p):
        return pltpu.make_async_remote_copy(
            src_ref=c_all.at[c, pl.ds(spots[p] * rows, rows), :], dst_ref=out_ref.at[:, cols(spot, c)],
            send_sem=c_send.at[c, p], recv_sem=c_recv.at[c, p],
            device_id={"row": peers[p]}, device_id_type=MESH)

    def local_result(c):
        return pltpu.make_async_copy(
            c_all.at[c, pl.ds(spot * rows, rows), :], out_ref.at[:, cols(spot, c)], c_local.at[c])

    barrier = pltpu.get_barrier_semaphore()
    for p in range(3):
        pl.semaphore_signal(barrier, inc=1, device_id={"row": peers[p]}, device_id_type=MESH)

    @pl.when(has_below)
    def _():
        pl.semaphore_signal(barrier, inc=1, device_id={"row": me - QUAD}, device_id_type=MESH)

    @pl.when(has_above)
    def _():
        pl.semaphore_signal(barrier, inc=1, device_id={"row": me + QUAD}, device_id_type=MESH)

    pl.semaphore_wait(barrier, 3 + has_below.astype(jnp.int32) + has_above.astype(jnp.int32))

    @pl.loop(0, chunks)
    def _(c):
        local_b(c).start()
        for p in range(3):
            quad_b(c, p).start()

    local_a().start()
    quad_a(0).start()

    @pl.loop(0, chunks)
    def _(c):
        local_b(c).wait()
        for p in range(3):
            quad_b(c, p).wait_recv()

        @pl.when(has_above)
        def _():
            along(c, layer, 1).start()

        @pl.when(has_below)
        def _():
            along(c, layer, 0).start()

    quad_a(1).start()

    def forward(c):
        for d in range(1, layers - 1):
            @pl.when((layer >= d) & has_above)
            def _():
                along(c, layer - d, 1).wait_recv()
                along(c, layer - d, 1).start()

            @pl.when((layer + d < layers) & has_below)
            def _():
                along(c, layer + d, 0).wait_recv()
                along(c, layer + d, 0).start()

    def compute(c):
        @pl.loop(0, layers)
        def _(owner):
            from_below, from_above = owner < layer, owner > layer
            passed_on = (from_below & has_above) | (from_above & has_below)

            @pl.when((from_below | from_above) & jnp.logical_not(passed_on))
            def _():
                along(c, owner, 0).wait_recv()

        @pl.loop(0, QUAD)
        def _(s):
            total = jnp.dot(a_all[s], b_all[c], preferred_element_type=jnp.float32)
            denominator = row_ref[s] + col_ref[c]
            at = pl.ds(pl.multiple_of(s * rows, rows), rows)
            c_all[c, at, :] = (total / denominator).astype(jnp.bfloat16)

        for p in (1, 2, 0):
            result(c, p).start()
        local_result(c).start()

    lag = 2

    @pl.loop(0, lag)
    def _(c):
        forward(c)

    local_a().wait()
    quad_a(1).wait_recv()
    quad_a(2).start()
    quad_a(0).wait_recv()
    quad_a(2).wait_recv()

    @pl.loop(lag, chunks + lag)
    def _(c):
        @pl.when(c < chunks)
        def _():
            forward(c)
        compute(c - lag)

    for p in range(3):
        quad_a(p).wait_send()

    @pl.loop(0, chunks)
    def _(c):
        local_result(c).wait()
        for p in range(3):
            quad_b(c, p).wait_send()
            result(c, p).wait()

        @pl.loop(0, layers)
        def _(owner):
            @pl.when((owner <= layer) & has_above)
            def _():
                along(c, owner, 1).wait_send()

            @pl.when((owner >= layer) & has_below)
            def _():
                along(c, owner, 0).wait_send()


def shards(amplitudes, integrals, occupied_energy, virtual_energy, pair_irrep):
    devices = lax.axis_size("row")
    layers = devices // QUAD
    rows, columns = amplitudes.shape
    depth = integrals.shape[0] * devices
    quarter = columns // QUAD
    width = 256
    chunks = quarter // width
    position = lax.axis_index("row")
    pair_energy = pair_energies(occupied_energy, virtual_energy, pair_irrep)
    row_energy = lax.dynamic_slice_in_dim(pair_energy, position // QUAD * QUAD * rows, QUAD * rows)
    col_energy = lax.dynamic_slice_in_dim(pair_energy, position % QUAD * quarter, quarter)
    dma = pltpu.SemaphoreType.DMA
    return pl.pallas_call(
        functools.partial(kernel, layers, chunks),
        out_shape=jax.ShapeDtypeStruct((rows, columns), jnp.bfloat16),
        in_specs=[pl.BlockSpec(memory_space=pl.ANY)] * 2 + [pl.BlockSpec(memory_space=pltpu.VMEM)] * 2,
        out_specs=pl.BlockSpec(memory_space=pl.ANY),
        scratch_shapes=[
            pltpu.VMEM((QUAD, rows, depth), jnp.bfloat16),
            pltpu.VMEM((chunks, depth, width), jnp.bfloat16),
            pltpu.VMEM((chunks, QUAD * rows, width), jnp.bfloat16),
            dma((1 + chunks,)),
            dma((chunks, 3)),
            dma((chunks, 3)),
            dma((3,)),
            dma((3,)),
            dma((2, chunks, layers)),
            dma((chunks, layers)),
            dma((chunks, 3)),
            dma((chunks, 3)),
            dma((chunks,)),
        ],
        compiler_params=pltpu.CompilerParams(
            collective_id=0, has_side_effects=True, vmem_limit_bytes=58 * 1024 * 1024),
        cost_estimate=pl.CostEstimate(
            flops=2 * rows * depth * columns, bytes_accessed=6 * rows * columns, transcendentals=0),
    )(amplitudes, integrals, row_energy.reshape(QUAD, rows, 1), col_energy.reshape(chunks, 1, width))


def solution(mesh):
    in_specs = (P(("grp", "row"), None), P(("grp", "row"), None), P(), P(), P("grp"))
    out_specs = P(("grp", "row"), None)
    return jax.shard_map(shards, mesh=mesh, in_specs=in_specs, out_specs=out_specs, check_vma=False)
```

time: 1030 us -> 350 us (0.34)
  waiting for transfers between devices: 652 us -> 0 us
  Pallas kernels: 0 us -> 340 us
  blocking collectives: 182 us -> 0 us
  starting transfers between devices: 86.2 us -> 0 us
  local copies, waits for them, and re-layouts: 66.9 us -> 7.38 us
  matrix products: 37.8 us -> 0 us
    all_to_all x2 -> x0, waiting for transfers between devices: 652 us -> none  [the longest x1 333 us: shards(): lax.all_to_all(tile_out, 'row', split_axis=0, concat_axis=0, tiled=True)]
    pallas_call x0 -> x1, Pallas kernels: none -> 340 us  [shards(): pl.pallas_call(functools.partial(kernel, layers, chunks), out_shape=jax.S...]
    all_to_all x1 -> x0, blocking collectives: 182 us -> none  [shards(): lax.all_to_all(finished, 'row', split_axis=0, concat_axis=0, tiled=True)]
    all_to_all x2 -> x0, starting transfers between devices: 86.2 us -> none  [the longest x1 78.8 us: shards(): lax.all_to_all(tile_out, 'row', split_axis=0, concat_axis=0, tiled=True)]
    broadcast_in_dim x4 -> x0, local copies, waits for them, and re-layouts: 47.7 us -> none  [the longest x2 34.1 us: shards(): jnp.broadcast_to(reshaped[:, None], (layer_count, block_count, panel_coun...]
    dot_general x1 -> x0, matrix products: 37.8 us -> none  [shards(): jnp.dot(row_panel, integral_slab, preferred_element_type=jnp.float32)]
  transfers between devices with their start and end apart: 2 -> 0, of which waited for: 2 -> 0; matrix products, arithmetic and copies ran while one was open for 1% -> 0% of each run, Pallas kernels for 0% -> 0%
where the time goes in v1:
time: 350 us; the launch traced here: 349 us
  Pallas kernels  340 us (97%)
  local copies, waits for them, and re-layouts  7.38 us (2%)
    pallas_call x1, Pallas kernels, shards(): pl.pallas_call(functools.partial(kernel, layers, chunks), out_shape=jax.S...  340 us

profile of v1, /device:TPU:0, one launch (start us, length us, event | category | flops | bytes accessed | tf_op | source)
XLA Modules:
  0.0 349.2 jit_solution(12831723820294885692)
XLA Ops:
  0.0 0.7 fusion
  0.7 0.8 multiply_reduce_fusion
  1.5 0.7 broadcast_add_fusion
  2.1 0.1 copy.7
  2.2 0.1 add.25
  2.3 0.1 fusion.1
  2.4 0.6 reshape.35.col_ref
  3.0 1.5 reshape.36.row_ref
  4.5 339.6 %shard_map.55 = bf16[384,6144]{1,0:T(8,128)(2,1)} custom-call(bf16[384,6144]{1,0:T(8,128)(2,1)} %a_ref.1, bf16[384,6144]{1,0:T(8,128)(2,1)} %b_ref.1, f32[4,384,1]{2,1,0:T(8,128)} %reshape.36.row_ref, f32[6,1,256]{2,1,0:T(1,128)} %reshape.35.col_ref), custom_call_target="tpu_custom_call" | custom-call | flops 28991029248 | bytes 14155776 | tf_op jit(solution)/shard_map/pallas_call | solution.py:203
  344.1 5.1 %copy.10 = bf16[384,6144]{1,0:T(8,128)(2,1)} copy(bf16[384,6144]{1,0:T(8,128)(2,1)} %shard_map.55) | data formatting | bytes 9437184

commit v2 on v1

v2 whole, which is shorter than its diff:
```python
import functools
import jax
import jax.numpy as jnp
from jax import lax
from jax.experimental import pallas as pl
from jax.experimental.pallas import tpu as pltpu
from jax.sharding import PartitionSpec as P

QUAD = 4
MESH = pl.DeviceIdType.MESH


def pair_energies(occupied_energy, virtual_energy, pair_irrep):
    labels = jnp.arange(virtual_energy.shape[0])
    onehot = (pair_irrep[:, None] == labels[None, :]).astype(jnp.float32)
    virtual = jnp.sum(onehot[:, :, None] * virtual_energy[None, :, :], axis=1)
    return (virtual + occupied_energy[:, None]).reshape(-1)


def kernel(layers, chunks, shed, a_ref, b_ref, row_ref, col_ref, out_ref, a_all, b_all, c_all,
           a_shed, c_shed, local_sem, bq_send, bq_recv, a_send, a_recv, z_send, z_recv, c_send, c_recv,
           c_local, az_send, az_recv, as_send, as_recv, cz_send, cz_recv, d_send, d_recv, d_local):
    rows = a_ref.shape[0]
    part = rows // 2
    width = b_all.shape[2]
    quarter = chunks * width
    layer_rows = QUAD * rows
    me = lax.axis_index("row")
    layer, spot = me // QUAD, me % QUAD
    half, core = spot // 2, spot % 2
    spots = ((half * 2) + (1 - core), (1 - half) * 2 + core, (1 - half) * 2 + (1 - core))
    peers = [layer * QUAD + s for s in spots]
    has_below, has_above = layer > 0, layer < layers - 1
    is_end = (layer == 0) | (layer == layers - 1)
    is_helper = (layer == 1) | (layer == layers - 2)
    upper = layer * 2 // layers
    depth = layer + upper * (layers - 1 - 2 * layer)
    mate = me + QUAD * (1 - 2 * upper) * (1 - 2 * depth)

    def local_a():
        return pltpu.make_async_copy(a_ref, a_all.at[spot], local_sem.at[0])

    def cols(owner, c):
        return pl.ds(pl.multiple_of(owner * quarter + c * width, width), width)

    def remote(src, dst, send, recv, device):
        return pltpu.make_async_remote_copy(
            src_ref=src, dst_ref=dst, send_sem=send, recv_sem=recv,
            device_id={"row": device}, device_id_type=MESH)

    def local_b(c):
        return pltpu.make_async_copy(
            b_ref.at[:, cols(spot, c)], b_all.at[c, pl.ds(me * rows, rows), :], local_sem.at[1 + c])

    def quad_b(c, p):
        return remote(b_ref.at[:, cols(spots[p], c)], b_all.at[c, pl.ds(me * rows, rows), :],
                      bq_send.at[c, p], bq_recv.at[c, p], peers[p])

    def quad_a(p):
        if p == 2:
            return remote(a_all.at[spots[1]], a_all.at[spots[1]], a_send.at[p], a_recv.at[p], peers[0])
        return remote(a_ref, a_all.at[spot], a_send.at[p], a_recv.at[p], peers[p])

    def along(c, owner, up):
        block = b_all.at[c, pl.ds(owner * layer_rows, layer_rows), :]
        return remote(block, block, z_send.at[up, c, owner], z_recv.at[c, owner],
                      me + QUAD if up else me - QUAD)

    def result(c, p):
        return remote(c_all.at[c, pl.ds(spots[p] * rows, rows), :], out_ref.at[:, cols(spot, c)],
                      c_send.at[c, p], c_recv.at[c, p], peers[p])

    def local_result(c):
        return pltpu.make_async_copy(
            c_all.at[c, pl.ds(spot * rows, rows), :], out_ref.at[:, cols(spot, c)], c_local.at[c])

    def piece(u):
        return pl.ds(u * part, part)

    def shed_z(k):
        u = 1 if k == 0 else 0
        src = a_all.at[spots[1], piece(u), :] if k == 2 else a_ref.at[piece(u), :]
        return remote(src, a_shed.at[spots[1] if k == 2 else spot, piece(u), :],
                      az_send.at[k], az_recv.at[k], mate)

    def shed_quad(k):
        at = a_shed.at[spot if k < 3 else spots[1], piece((1, 1, 0, 1, 0)[k]), :]
        return remote(at, at, as_send.at[k], as_recv.at[k], peers[1] if k == 0 else peers[0])

    order = ((3, 1), (0, 1), (3, 0), (0, 0), (1, 1), (2, 1), (1, 0), (2, 0))

    def spot_of(p):
        return spot if p == 3 else spots[p]

    def at_rows(p, u):
        return pl.ds(spot_of(p) * rows + u * part, part)

    def back(o, h):
        at = at_rows(*order[h])
        return remote(c_shed.at[o, at, :], c_all.at[o, at, :], cz_send.at[o, h], cz_recv.at[o, h], mate)

    def deal(o, h):
        p, u = order[h]
        src, dst = c_all.at[o, at_rows(p, u), :], out_ref.at[piece(u), cols(spot, o)]
        if p == 3:
            return pltpu.make_async_copy(src, dst, d_local.at[o, u])
        return remote(src, dst, d_send.at[o, u, p], d_recv.at[o, u, p], peers[p])

    barrier = pltpu.get_barrier_semaphore()
    for p in range(3):
        pl.semaphore_signal(barrier, inc=1, device_id={"row": peers[p]}, device_id_type=MESH)

    @pl.when(has_below)
    def _():
        pl.semaphore_signal(barrier, inc=1, device_id={"row": me - QUAD}, device_id_type=MESH)

    @pl.when(has_above)
    def _():
        pl.semaphore_signal(barrier, inc=1, device_id={"row": me + QUAD}, device_id_type=MESH)

    pl.semaphore_wait(barrier, 3 + has_below.astype(jnp.int32) + has_above.astype(jnp.int32))

    @pl.loop(0, chunks)
    def _(c):
        local_b(c).start()
        for p in range(3):
            quad_b(c, p).start()

    local_a().start()
    quad_a(0).start()

    def goes_up(c):
        return has_above & ((layer < layers - 2) | (c >= shed))

    def goes_down(c):
        return has_below & ((layer > 1) | (c >= shed))

    def due(c):
        return jnp.logical_not(is_end) | (c >= shed)

    @pl.loop(0, chunks)
    def _(c):
        local_b(c).wait()
        for p in range(3):
            quad_b(c, p).wait_recv()

        @pl.when(goes_up(c))
        def _():
            along(c, layer, 1).start()

        @pl.when(goes_down(c))
        def _():
            along(c, layer, 0).start()

    quad_a(1).start()

    def forward(d, c):
        @pl.when((layer >= d) & goes_up(c))
        def _():
            along(c, layer - d, 1).wait_recv()
            along(c, layer - d, 1).start()

        @pl.when((layer + d < layers) & goes_down(c))
        def _():
            along(c, layer + d, 0).wait_recv()
            along(c, layer + d, 0).start()

    def compute(c):
        @pl.loop(0, layers)
        def _(owner):
            from_below, from_above = owner < layer, owner > layer
            passed_on = (from_below & goes_up(c)) | (from_above & goes_down(c))

            @pl.when((from_below | from_above) & jnp.logical_not(passed_on))
            def _():
                along(c, owner, 0).wait_recv()

        @pl.loop(0, QUAD)
        def _(s):
            total = jnp.dot(a_all[s], b_all[c], preferred_element_type=jnp.float32)
            denominator = row_ref[0, s] + col_ref[c]
            at = pl.ds(pl.multiple_of(s * rows, rows), rows)
            c_all[c, at, :] = (total / denominator).astype(jnp.bfloat16)

        for p in (1, 2, 0):
            result(c, p).start()
        local_result(c).start()

    def compute_shed(h):
        p, u = order[h]

        @pl.loop(0, shed)
        def _(o):
            total = jnp.dot(a_shed[spot_of(p), piece(u), :], b_all[o], preferred_element_type=jnp.float32)
            denominator = row_ref[1, spot_of(p), piece(u), :] + col_ref[o]
            c_shed[o, at_rows(p, u), :] = (total / denominator).astype(jnp.bfloat16)
            back(o, h).start()

    lag = 2
    last = layers - 2

    for d in range(1, last):
        @pl.loop(0, chunks)
        def _(c):
            forward(d, c)

    @pl.when(is_end)
    def _():
        @pl.loop(0, chunks)
        def _(c):
            @pl.when(has_above)
            def _():
                along(c, layer, 1).wait_send()

            @pl.when(has_below)
            def _():
                along(c, layer, 0).wait_send()
        shed_z(0).start()

    @pl.loop(0, lag)
    def _(c):
        forward(last, c)

    local_a().wait()
    quad_a(1).wait_recv()
    quad_a(2).start()

    @pl.when(is_end)
    def _():
        shed_z(0).wait_send()
        shed_z(1).start()

    quad_a(0).wait_recv()
    quad_a(2).wait_recv()

    @pl.loop(lag, chunks + lag)
    def _(c):
        @pl.when(c < chunks)
        def _():
            forward(last, c)

        @pl.when(is_end & (c == chunks + lag - 1))
        def _():
            shed_z(1).wait_send()
            shed_z(2).start()

        @pl.when(is_helper & (c == lag + 1))
        def _():
            shed_z(0).wait_recv()
            shed_quad(0).start()
            shed_quad(1).start()

        @pl.when(due(c - lag))
        def _():
            compute(c - lag)

    @pl.when(is_helper)
    def _():
        shed_quad(1).wait_recv()
        compute_shed(0)
        compute_shed(1)
        shed_z(1).wait_recv()
        shed_quad(2).start()
        compute_shed(2)
        shed_quad(2).wait_recv()
        compute_shed(3)
        shed_quad(0).wait_recv()
        shed_quad(3).start()
        compute_shed(4)
        shed_quad(3).wait_recv()
        compute_shed(5)
        shed_z(2).wait_recv()
        shed_quad(4).start()
        compute_shed(6)
        shed_quad(4).wait_recv()
        compute_shed(7)
        for k in range(5):
            shed_quad(k).wait_send()
        for h in range(8):
            @pl.loop(0, shed)
            def _(o):
                back(o, h).wait_send()

    @pl.when(is_end)
    def _():
        for h in range(8):
            @pl.loop(0, shed)
            def _(o):
                back(o, h).wait_recv()
                deal(o, h).start()
        shed_z(2).wait_send()
        for h in range(8):
            @pl.loop(0, shed)
            def _(o):
                deal(o, h).wait()

    for p in range(3):
        quad_a(p).wait_send()

    @pl.loop(0, chunks)
    def _(c):
        for p in range(3):
            quad_b(c, p).wait_send()

        @pl.when(due(c))
        def _():
            local_result(c).wait()
            for p in range(3):
                result(c, p).wait()

        @pl.loop(0, layers)
        def _(owner):
            @pl.when((owner <= layer) & goes_up(c) & jnp.logical_not(is_end))
            def _():
                along(c, owner, 1).wait_send()

            @pl.when((owner >= layer) & goes_down(c) & jnp.logical_not(is_end))
            def _():
                along(c, owner, 0).wait_send()


def shards(amplitudes, integrals, occupied_energy, virtual_energy, pair_irrep):
    devices = lax.axis_size("row")
    layers = devices // QUAD
    rows, columns = amplitudes.shape
    depth = integrals.shape[0] * devices
    quarter = columns // QUAD
    width = 256
    chunks = quarter // width
    shed = chunks // 3
    position = lax.axis_index("row")
    pair_energy = pair_energies(occupied_energy, virtual_energy, pair_irrep)
    layer = position // QUAD
    upper = layer * 2 // layers
    depth_in = layer + upper * (layers - 1 - 2 * layer)
    mate = layer + (1 - 2 * upper) * (1 - 2 * depth_in)
    row_energy = jnp.stack([
        lax.dynamic_slice_in_dim(pair_energy, at * QUAD * rows, QUAD * rows) for at in (layer, mate)])
    col_energy = lax.dynamic_slice_in_dim(pair_energy, position % QUAD * quarter, quarter)
    dma = pltpu.SemaphoreType.DMA
    return pl.pallas_call(
        functools.partial(kernel, layers, chunks, shed),
        out_shape=jax.ShapeDtypeStruct((rows, columns), jnp.bfloat16),
        in_specs=[pl.BlockSpec(memory_space=pl.ANY)] * 2 + [pl.BlockSpec(memory_space=pltpu.VMEM)] * 2,
        out_specs=pl.BlockSpec(memory_space=pl.ANY),
        scratch_shapes=[
            pltpu.VMEM((QUAD, rows, depth), jnp.bfloat16),
            pltpu.VMEM((chunks, depth, width), jnp.bfloat16),
            pltpu.VMEM((chunks, QUAD * rows, width), jnp.bfloat16),
            pltpu.VMEM((QUAD, rows, depth), jnp.bfloat16),
            pltpu.VMEM((shed, QUAD * rows, width), jnp.bfloat16),
            dma((1 + chunks,)),
            dma((chunks, 3)),
            dma((chunks, 3)),
            dma((3,)),
            dma((3,)),
            dma((2, chunks, layers)),
            dma((chunks, layers)),
            dma((chunks, 3)),
            dma((chunks, 3)),
            dma((chunks,)),
            dma((3,)),
            dma((3,)),
            dma((5,)),
            dma((5,)),
            dma((shed, 8)),
            dma((shed, 8)),
            dma((shed, 2, 3)),
            dma((shed, 2, 3)),
            dma((shed, 2)),
        ],
        compiler_params=pltpu.CompilerParams(
            collective_id=0, has_side_effects=True, vmem_limit_bytes=63 * 1024 * 1024),
        cost_estimate=pl.CostEstimate(
            flops=2 * rows * depth * columns, bytes_accessed=6 * rows * columns, transcendentals=0),
    )(amplitudes, integrals, row_energy.reshape(2, QUAD, rows, 1), col_energy.reshape(chunks, 1, width))


def solution(mesh):
    in_specs = (P(("grp", "row"), None), P(("grp", "row"), None), P(), P(), P("grp"))
    out_specs = P(("grp", "row"), None)
    return jax.shard_map(shards, mesh=mesh, in_specs=in_specs, out_specs=out_specs, check_vma=False)
```

time: 350 us -> 308 us (0.88)
  Pallas kernels: 340 us -> 298 us
    pallas_call x1, Pallas kernels: 340 us -> 298 us  [shards(): pl.pallas_call(functools.partial(kernel, layers, chunks, shed), out_shape...]
where the time goes in v2:
time: 308 us
  Pallas kernels  298 us (97%)
  local copies, waits for them, and re-layouts  7.58 us (2%)
    pallas_call x1, Pallas kernels, shards(): pl.pallas_call(functools.partial(kernel, layers, chunks, shed), out_shape...  298 us

profile of v2, /device:TPU:0, one launch (start us, length us, event | category | flops | bytes accessed | tf_op | source)
XLA Modules:
  0.0 308.0 jit_solution(1733220222115929218)
XLA Ops:
  0.0 0.7 fusion
  0.7 0.8 multiply_reduce_fusion
  1.5 0.7 broadcast_add_fusion
  2.1 0.1 copy.9
  2.2 0.1 add.35
  2.3 0.1 fusion.1
  2.4 0.6 reshape.36.col_ref
  3.0 1.7 copy.10.row_ref
  4.7 298.2 %shard_map.55 = bf16[384,6144]{1,0:T(8,128)(2,1)} custom-call(bf16[384,6144]{1,0:T(8,128)(2,1)} %a_ref.1, bf16[384,6144]{1,0:T(8,128)(2,1)} %b_ref.1, f32[2,4,384,1]{3,2,1,0:T(8,128)} %copy.10.row_ref, f32[6,1,256]{2,1,0:T(1,128)} %reshape.36.col_ref), custom_call_target="tpu_custom_call" | custom-call | flops 28991029248 | bytes 14155776 | tf_op jit(solution)/shard_map/pallas_call | solution.py:341
  302.9 5.1 %copy.12 = bf16[384,6144]{1,0:T(8,128)(2,1)} copy(bf16[384,6144]{1,0:T(8,128)(2,1)} %shard_map.55) | data formatting | bytes 9437184
  (3 shorter events, 0.0 us)

commit v3 on v2

--- a/solution.py
+++ b/solution.py
@@ -8,20 +8,16 @@
 
 QUAD = 4
 MESH = pl.DeviceIdType.MESH
-
-
-def pair_energies(occupied_energy, virtual_energy, pair_irrep):
-    labels = jnp.arange(virtual_energy.shape[0])
-    onehot = (pair_irrep[:, None] == labels[None, :]).astype(jnp.float32)
-    virtual = jnp.sum(onehot[:, :, None] * virtual_energy[None, :, :], axis=1)
-    return (virtual + occupied_energy[:, None]).reshape(-1)
-
-
-def kernel(layers, chunks, shed, a_ref, b_ref, row_ref, col_ref, out_ref, a_all, b_all, c_all,
-           a_shed, c_shed, local_sem, bq_send, bq_recv, a_send, a_recv, z_send, z_recv, c_send, c_recv,
-           c_local, az_send, az_recv, as_send, as_recv, cz_send, cz_recv, d_send, d_recv, d_local):
+UPPER, LOWER, LOWER_A, LOWER_B = (3, 3), (0, 3), (0, 2), (2, 1)
+ORDER = ((3, UPPER), (0, UPPER), (3, LOWER), (0, LOWER), (1, UPPER), (2, UPPER),
+         (1, LOWER_A), (2, LOWER_A), (1, LOWER_B), (2, LOWER_B))
+
+
+def kernel(layers, chunks, shed, a_ref, b_ref, occupied_ref, virtual_ref, irrep_ref, out_ref, a_all,
+           b_all, c_all, a_shed, c_shed, row_ref, col_ref, local_sem, bq_send, bq_recv, a_send, a_recv, z_send, z_recv, c_send, c_recv,
+           c_local, az_send, az_recv, as_send, as_recv, cz_send, cz_recv, d_send, d_recv):
     rows = a_ref.shape[0]
-    part = rows // 2
+    part = rows // 6
     width = b_all.shape[2]
     quarter = chunks * width
     layer_rows = QUAD * rows
@@ -75,36 +71,35 @@
             c_all.at[c, pl.ds(spot * rows, rows), :], out_ref.at[:, cols(spot, c)], c_local.at[c])
 
     def piece(u):
-        return pl.ds(u * part, part)
+        return pl.ds(u[0] * part, u[1] * part)
 
     def shed_z(k):
-        u = 1 if k == 0 else 0
-        src = a_all.at[spots[1], piece(u), :] if k == 2 else a_ref.at[piece(u), :]
-        return remote(src, a_shed.at[spots[1] if k == 2 else spot, piece(u), :],
+        u = (UPPER, LOWER, LOWER_A, LOWER_B)[k]
+        src = a_all.at[spots[1], piece(u), :] if k > 1 else a_ref.at[piece(u), :]
+        return remote(src, a_shed.at[spots[1] if k > 1 else spot, piece(u), :],
                       az_send.at[k], az_recv.at[k], mate)
 
     def shed_quad(k):
-        at = a_shed.at[spot if k < 3 else spots[1], piece((1, 1, 0, 1, 0)[k]), :]
+        u = (UPPER, UPPER, LOWER, UPPER, LOWER_A, LOWER_B)[k]
+        at = a_shed.at[spot if k < 3 else spots[1], piece(u), :]
         return remote(at, at, as_send.at[k], as_recv.at[k], peers[1] if k == 0 else peers[0])
-
-    order = ((3, 1), (0, 1), (3, 0), (0, 0), (1, 1), (2, 1), (1, 0), (2, 0))
 
     def spot_of(p):
         return spot if p == 3 else spots[p]
 
     def at_rows(p, u):
-        return pl.ds(spot_of(p) * rows + u * part, part)
+        return pl.ds(spot_of(p) * rows + u[0] * part, u[1] * part)
 
     def back(o, h):
-        at = at_rows(*order[h])
+        at = at_rows(*ORDER[h])
         return remote(c_shed.at[o, at, :], c_all.at[o, at, :], cz_send.at[o, h], cz_recv.at[o, h], mate)
 
     def deal(o, h):
-        p, u = order[h]
+        p, u = ORDER[h]
         src, dst = c_all.at[o, at_rows(p, u), :], out_ref.at[piece(u), cols(spot, o)]
         if p == 3:
-            return pltpu.make_async_copy(src, dst, d_local.at[o, u])
-        return remote(src, dst, d_send.at[o, u, p], d_recv.at[o, u, p], peers[p])
+            return pltpu.make_async_copy(src, dst, d_send.at[o, h])
+        return remote(src, dst, d_send.at[o, h], d_recv.at[o, h], peers[p])
 
     barrier = pltpu.get_barrier_semaphore()
     for p in range(3):
@@ -125,6 +120,10 @@
         local_b(c).start()
         for p in range(3):
             quad_b(c, p).start()
+
+    @pl.when(is_end)
+    def _():
+        shed_z(0).start()
 
     local_a().start()
     quad_a(0).start()
@@ -178,8 +177,8 @@
         @pl.loop(0, QUAD)
         def _(s):
             total = jnp.dot(a_all[s], b_all[c], preferred_element_type=jnp.float32)
-            denominator = row_ref[0, s] + col_ref[c]
             at = pl.ds(pl.multiple_of(s * rows, rows), rows)
+            denominator = row_ref[0, at, :] + col_ref[c]
             c_all[c, at, :] = (total / denominator).astype(jnp.bfloat16)
 
         for p in (1, 2, 0):
@@ -187,14 +186,41 @@
         local_result(c).start()
 
     def compute_shed(h):
-        p, u = order[h]
+        p, u = ORDER[h]
 
         @pl.loop(0, shed)
         def _(o):
             total = jnp.dot(a_shed[spot_of(p), piece(u), :], b_all[o], preferred_element_type=jnp.float32)
-            denominator = row_ref[1, spot_of(p), piece(u), :] + col_ref[o]
+            denominator = row_ref[1, at_rows(p, u), :] + col_ref[o]
             c_shed[o, at_rows(p, u), :] = (total / denominator).astype(jnp.bfloat16)
             back(o, h).start()
+
+    irreps, virtuals = virtual_ref.shape
+    label = lax.broadcasted_iota(jnp.int32, (irreps, virtuals), 0)
+    diagonal = (lax.broadcasted_iota(jnp.int32, (virtuals, virtuals), 0)
+                == lax.broadcasted_iota(jnp.int32, (virtuals, virtuals), 1))
+
+    def energies(orbital):
+        chosen = jnp.where(label == irrep_ref[orbital], virtual_ref[...], 0.0)
+        return jnp.sum(chosen, axis=0, keepdims=True) + occupied_ref[orbital]
+
+    orbitals = layer_rows // virtuals
+    for which, owner in enumerate((layer, layer + (1 - 2 * upper) * (1 - 2 * depth))):
+        @pl.when((which == 0) | is_helper)
+        def _():
+            @pl.loop(0, orbitals)
+            def _(i):
+                along_lanes = jnp.broadcast_to(energies(owner * orbitals + i), (virtuals, virtuals))
+                at = pl.ds(pl.multiple_of(i * virtuals, virtuals), virtuals)
+                row_ref[which, at, :] = jnp.sum(jnp.where(diagonal, along_lanes, 0.0), axis=1, keepdims=True)
+
+    per_chunk = width // virtuals
+
+    @pl.loop(0, chunks)
+    def _(c):
+        for k in range(per_chunk):
+            col_ref[c, :, k * virtuals:(k + 1) * virtuals] = energies(
+                (spot * chunks + c) * per_chunk + k)
 
     lag = 2
     last = layers - 2
@@ -208,6 +234,10 @@
     def _():
         @pl.loop(0, chunks)
         def _(c):
+            @pl.when(c == chunks - 1)
+            def _():
+                shed_z(1).start()
+
             @pl.when(has_above)
             def _():
                 along(c, layer, 1).wait_send()
@@ -215,7 +245,6 @@
             @pl.when(has_below)
             def _():
                 along(c, layer, 0).wait_send()
-        shed_z(0).start()
 
     @pl.loop(0, lag)
     def _(c):
@@ -225,11 +254,6 @@
     quad_a(1).wait_recv()
     quad_a(2).start()
 
-    @pl.when(is_end)
-    def _():
-        shed_z(0).wait_send()
-        shed_z(1).start()
-
     quad_a(0).wait_recv()
     quad_a(2).wait_recv()
 
@@ -239,10 +263,10 @@
         def _():
             forward(last, c)
 
-        @pl.when(is_end & (c == chunks + lag - 1))
-        def _():
-            shed_z(1).wait_send()
+        @pl.when(is_end & (c == chunks + lag - 2))
+        def _():
             shed_z(2).start()
+            shed_z(3).start()
 
         @pl.when(is_helper & (c == lag + 1))
         def _():
@@ -269,27 +293,29 @@
         compute_shed(4)
         shed_quad(3).wait_recv()
         compute_shed(5)
-        shed_z(2).wait_recv()
-        shed_quad(4).start()
-        compute_shed(6)
-        shed_quad(4).wait_recv()
-        compute_shed(7)
-        for k in range(5):
+        for k in (2, 3):
+            shed_z(k).wait_recv()
+            shed_quad(k + 2).start()
+            compute_shed(2 * k + 2)
+            shed_quad(k + 2).wait_recv()
+            compute_shed(2 * k + 3)
+        for k in range(6):
             shed_quad(k).wait_send()
-        for h in range(8):
+        for h in range(len(ORDER)):
             @pl.loop(0, shed)
             def _(o):
                 back(o, h).wait_send()
 
     @pl.when(is_end)
     def _():
-        for h in range(8):
+        for h in range(len(ORDER)):
             @pl.loop(0, shed)
             def _(o):
                 back(o, h).wait_recv()
                 deal(o, h).start()
-        shed_z(2).wait_send()
-        for h in range(8):
+        for k in range(4):
+            shed_z(k).wait_send()
+        for h in range(len(ORDER)):
             @pl.loop(0, shed)
             def _(o):
                 deal(o, h).wait()
@@ -328,20 +354,12 @@
     width = 256
     chunks = quarter // width
     shed = chunks // 3
-    position = lax.axis_index("row")
-    pair_energy = pair_energies(occupied_energy, virtual_energy, pair_irrep)
-    layer = position // QUAD
-    upper = layer * 2 // layers
-    depth_in = layer + upper * (layers - 1 - 2 * layer)
-    mate = layer + (1 - 2 * upper) * (1 - 2 * depth_in)
-    row_energy = jnp.stack([
-        lax.dynamic_slice_in_dim(pair_energy, at * QUAD * rows, QUAD * rows) for at in (layer, mate)])
-    col_energy = lax.dynamic_slice_in_dim(pair_energy, position % QUAD * quarter, quarter)
     dma = pltpu.SemaphoreType.DMA
     return pl.pallas_call(
         functools.partial(kernel, layers, chunks, shed),
         out_shape=jax.ShapeDtypeStruct((rows, columns), jnp.bfloat16),
-        in_specs=[pl.BlockSpec(memory_space=pl.ANY)] * 2 + [pl.BlockSpec(memory_space=pltpu.VMEM)] * 2,
+        in_specs=[pl.BlockSpec(memory_space=space) for space in (
+            pl.ANY, pl.ANY, pltpu.SMEM, pltpu.VMEM, pltpu.SMEM)],
         out_specs=pl.BlockSpec(memory_space=pl.ANY),
         scratch_shapes=[
             pltpu.VMEM((QUAD, rows, depth), jnp.bfloat16),
@@ -349,6 +367,8 @@
             pltpu.VMEM((chunks, QUAD * rows, width), jnp.bfloat16),
             pltpu.VMEM((QUAD, rows, depth), jnp.bfloat16),
             pltpu.VMEM((shed, QUAD * rows, width), jnp.bfloat16),
+            pltpu.VMEM((2, QUAD * rows, 1), jnp.float32),
+            pltpu.VMEM((chunks, 1, width), jnp.float32),
             dma((1 + chunks,)),
             dma((chunks, 3)),
             dma((chunks, 3)),
@@ -359,21 +379,20 @@
             dma((chunks, 3)),
             dma((chunks, 3)),
             dma((chunks,)),
-            dma((3,)),
-            dma((3,)),
-            dma((5,)),
-            dma((5,)),
-            dma((shed, 8)),
-            dma((shed, 8)),
-            dma((shed, 2, 3)),
-            dma((shed, 2, 3)),
-            dma((shed, 2)),
+            dma((4,)),
+            dma((4,)),
+            dma((6,)),
+            dma((6,)),
+            dma((shed, len(ORDER))),
+            dma((shed, len(ORDER))),
+            dma((shed, len(ORDER))),
+            dma((shed, len(ORDER))),
         ],
         compiler_params=pltpu.CompilerParams(
             collective_id=0, has_side_effects=True, vmem_limit_bytes=63 * 1024 * 1024),
         cost_estimate=pl.CostEstimate(
             flops=2 * rows * depth * columns, bytes_accessed=6 * rows * columns, transcendentals=0),
-    )(amplitudes, integrals, row_energy.reshape(2, QUAD, rows, 1), col_energy.reshape(chunks, 1, width))
+    )(amplitudes, integrals, occupied_energy, virtual_energy, pair_irrep)
 
 
 def solution(mesh):

time: 308 us -> 288 us (0.935)
  Pallas kernels: 298 us -> 283 us
    pallas_call x1, Pallas kernels: 298 us -> 283 us  [shards(): pl.pallas_call(functools.partial(kernel, layers, chunks, shed), out_shape...]
where the time goes in v3:
time: 288 us
  Pallas kernels  283 us (98%)
  local copies, waits for them, and re-layouts  5.05 us (2%)
    pallas_call x1, Pallas kernels, shards(): pl.pallas_call(functools.partial(kernel, layers, chunks, shed), out_shape...  283 us

profile of v3, /device:TPU:0, one launch (start us, length us, event | category | flops | bytes accessed | tf_op | source)
XLA Modules:
  0.0 288.2 jit_solution(10834791611644940389)
XLA Ops:
  0.0 283.2 %shard_map.55 = bf16[384,6144]{1,0:T(8,128)(2,1)} custom-call(bf16[384,6144]{1,0:T(8,128)(2,1)} %a_ref.1, bf16[384,6144]{1,0:T(8,128)(2,1)} %b_ref.1, f32[96]{0:T(128)} %occupied_ref.1, f32[8,64]{1,0:T(8,128)} %virtual_ref.1, s32[96]{0:T(128)} %irrep_ref.1), custom_call_target="tpu_custom_call" | custom-call | flops 28991029248 | bytes 14155776 | tf_op jit(solution)/shard_map/pallas_call | solution.py:358
  283.2 5.1 %copy.7 = bf16[384,6144]{1,0:T(8,128)(2,1)} copy(bf16[384,6144]{1,0:T(8,128)(2,1)} %shard_map.55) | data formatting | bytes 9437184

commit v4 on v3

--- a/solution.py
+++ b/solution.py
@@ -164,6 +164,13 @@
             along(c, layer + d, 0).wait_recv()
             along(c, layer + d, 0).start()
 
+    held = min(2, chunks - 1)
+
+    def send(c):
+        for p in (1, 2, 0):
+            result(c, p).start()
+        local_result(c).start()
+
     def compute(c):
         @pl.loop(0, layers)
         def _(owner):
@@ -181,9 +188,17 @@
             denominator = row_ref[0, at, :] + col_ref[c]
             c_all[c, at, :] = (total / denominator).astype(jnp.bfloat16)
 
-        for p in (1, 2, 0):
-            result(c, p).start()
-        local_result(c).start()
+        @pl.when(jnp.logical_not(is_helper) | (c > held))
+        def _():
+            send(c)
+
+        @pl.when(is_helper & (c == held))
+        def _():
+            shed_quad(0).wait_send()
+
+            @pl.loop(0, held + 1)
+            def _(k):
+                send(k)
 
     def compute_shed(h):
         p, u = ORDER[h]
@@ -254,6 +269,12 @@
     quad_a(1).wait_recv()
     quad_a(2).start()
 
+    @pl.when(is_helper)
+    def _():
+        shed_z(0).wait_recv()
+        shed_quad(0).start()
+        shed_quad(1).start()
+
     quad_a(0).wait_recv()
     quad_a(2).wait_recv()
 
@@ -267,12 +288,6 @@
         def _():
             shed_z(2).start()
             shed_z(3).start()
-
-        @pl.when(is_helper & (c == lag + 1))
-        def _():
-            shed_z(0).wait_recv()
-            shed_quad(0).start()
-            shed_quad(1).start()
 
         @pl.when(due(c - lag))
         def _():
@@ -299,7 +314,7 @@
             compute_shed(2 * k + 2)
             shed_quad(k + 2).wait_recv()
             compute_shed(2 * k + 3)
-        for k in range(6):
+        for k in range(1, 6):
             shed_quad(k).wait_send()
         for h in range(len(ORDER)):
             @pl.loop(0, shed)

time: 288 us -> 288 us (level)
  no operation moved by 1% of the time
where the time goes in v4:
time: 288 us
  Pallas kernels  283 us (98%)
  local copies, waits for them, and re-layouts  5.05 us (2%)
    pallas_call x1, Pallas kernels, shards(): pl.pallas_call(functools.partial(kernel, layers, chunks, shed), out_shape...  283 us

profile of v4, /device:TPU:0, one launch (start us, length us, event | category | flops | bytes accessed | tf_op | source)
XLA Modules:
  0.0 288.2 jit_solution(950734091952848211)
XLA Ops:
  0.0 283.2 %shard_map.55 = bf16[384,6144]{1,0:T(8,128)(2,1)} custom-call(bf16[384,6144]{1,0:T(8,128)(2,1)} %a_ref.1, bf16[384,6144]{1,0:T(8,128)(2,1)} %b_ref.1, f32[96]{0:T(128)} %occupied_ref.1, f32[8,64]{1,0:T(8,128)} %virtual_ref.1, s32[96]{0:T(128)} %irrep_ref.1), custom_call_target="tpu_custom_call" | custom-call | flops 28991029248 | bytes 14155776 | tf_op jit(solution)/shard_map/pallas_call | solution.py:373
  283.2 5.1 %copy.7 = bf16[384,6144]{1,0:T(8,128)(2,1)} copy(bf16[384,6144]{1,0:T(8,128)(2,1)} %shard_map.55) | data formatting | bytes 9437184
